TPU v7x, 256 devices: a whole 4x4x8 slice. The times are simulated.
256 devices in a mesh: dp: 2 (over core), pb: 8 (over z_hi, x), ta: 16 (over z_lo, y).
Axes of the slice: x: 4, y: 4, z: 8 (z_hi: 2, z_lo: 4; z = z_hi * 4 + z_lo), core: 2. Of those that a mesh axis runs over, the one named last changes fastest.
Arguments:
- fmap1: bfloat16 [16384, 256], P(('dp', 'pb'), 'ta'), parts along dimension 0, may hold values from -6 to 6
- fmap2: bfloat16 [65536, 256], P(('dp', 'ta'), 'pb'), parts along dimension 0, may hold values from -6 to 6
- cot0: bfloat16 [16384, 32768], P(('dp', 'pb'), 'ta'), parts along dimension 0, may hold values from -0.75 to 0.75
- cot1: bfloat16 [16384, 8192], P(('dp', 'pb'), 'ta'), parts along dimension 0, may hold values from -3 to 3
- cot2: bfloat16 [16384, 2048], P(('dp', 'pb'), 'ta'), parts along dimension 0, may hold values from -6 to 6
- cot3: bfloat16 [16384, 512], P(('dp', 'pb'), 'ta'), parts along dimension 0, may hold values from -20 to 20
Outputs:
- corr0: bfloat16 [16384, 32768], P(('dp', 'pb'), 'ta'), parts along dimension 0
- corr1: bfloat16 [16384, 8192], P(('dp', 'pb'), 'ta'), parts along dimension 0
- corr2: bfloat16 [16384, 2048], P(('dp', 'pb'), 'ta'), parts along dimension 0
- corr3: bfloat16 [16384, 512], P(('dp', 'pb'), 'ta'), parts along dimension 0
- grad_query: bfloat16 [16384, 256], P(('dp', 'pb'), 'ta'), parts along dimension 0
- grad_target: bfloat16 [65536, 256], P(('dp', 'ta'), 'pb'), parts along dimension 0
There are 2 independent parts, one for each index of `dp`. A program takes and returns all parts, laid end to end along the dimension named above; each array names one. Nothing has to cross between parts.
All inputs are finite; a program needn't handle non-finite values.
Results may differ from a plain program's by a relative error of at most 0.017.
Values may be sent and summed in bfloat16 or wider, within the bound.
A program may use at most 128 MiB of HBM per device.

v0:
```python
import math

import jax
import jax.numpy as jnp
from jax import lax
from jax.sharding import PartitionSpec as P

C = 256
W = 256


def pool_last(volume, height, across):
    lead = volume.shape[:-1]
    shaped = volume.reshape(lead + (height // 2, 2, across // 2, 2))
    return jnp.mean(shaped, axis=(-3, -1)).reshape(lead + (height * across // 4,))


def spread_last(coarse, height, across):
    lead = coarse.shape[:-1]
    shaped = coarse.reshape(lead + (height, 1, across, 1))
    shaped = jnp.broadcast_to(shaped, lead + (height, 2, across, 2))
    return 0.25 * shaped.reshape(lead + (height * across * 4,))


def combine_cotangents(first, second, third, fourth, height, across):
    merged = third.astype(jnp.float32) + spread_last(
        fourth.astype(jnp.float32), height // 8, across // 8
    )
    merged = second.astype(jnp.float32) + spread_last(merged, height // 4, across // 4)
    return first.astype(jnp.float32) + spread_last(merged, height // 2, across // 2)


def pair_product(left, right):
    return lax.dot_general(
        left, right, (((1,), (1,)), ((), ())), preferred_element_type=jnp.float32
    )


def body(fmap1, fmap2, cot0, cot1, cot2, cot3):
    factor = 1.0 / math.sqrt(C)
    query_full = lax.all_gather(fmap1, "ta", axis=1, tiled=True)
    target_full = lax.all_gather(fmap2, "pb", axis=1, tiled=True)
    height = target_full.shape[0] // W
    volume = pair_product(query_full, target_full) * factor
    levels = [volume.astype(jnp.bfloat16)]
    rows_now = height
    cols_now = W
    for level in range(3):
        volume = pool_last(volume, rows_now, cols_now)
        rows_now = rows_now // 2
        cols_now = cols_now // 2
        levels.append(volume.astype(jnp.bfloat16))
    weights = combine_cotangents(cot0, cot1, cot2, cot3, height, W).astype(jnp.bfloat16)
    channel = target_full
    grad_query = lax.psum_scatter(
        lax.dot_general(
            channel, weights, (((0,), (1,)), ((), ())), preferred_element_type=jnp.float32
        )
        * factor,
        "ta",
        scatter_dimension=0,
        tiled=True,
    )
    grad_query = grad_query.T.astype(jnp.bfloat16)
    channel = query_full
    grad_target = lax.psum_scatter(
        (
            lax.dot_general(
                channel, weights, (((0,), (0,)), ((), ())), preferred_element_type=jnp.float32
            )
            * factor
        ).astype(jnp.bfloat16),
        "pb",
        scatter_dimension=0,
        tiled=True,
    ).astype(jnp.float32)
    grad_target = grad_target.T.astype(jnp.bfloat16)
    return (levels[0], levels[1], levels[2], levels[3], grad_query, grad_target)


def solution(mesh):
    return jax.shard_map(
        body,
        mesh=mesh,
        in_specs=(
            P(("dp", "pb"), "ta"),
            P(("dp", "ta"), "pb"),
            P(("dp", "pb"), "ta"),
            P(("dp", "pb"), "ta"),
            P(("dp", "pb"), "ta"),
            P(("dp", "pb"), "ta"),
        ),
        out_specs=(
            P(("dp", "pb"), "ta"),
            P(("dp", "pb"), "ta"),
            P(("dp", "pb"), "ta"),
            P(("dp", "pb"), "ta"),
            P(("dp", "pb"), "ta"),
            P(("dp", "ta"), "pb"),
        ),
        check_vma=False,
    )
```

profile of v0, /device:TPU:32, one launch (start us, length us, event | category | flops | bytes accessed | tf_op | source)
XLA Modules:
  0.0 257.1 jit_solution(5799770484564390565)
XLA Ops:
  7.2 0.7 all-gather.2.cloned.1.call-update
  7.9 1.1 copy.27
  9.0 0.9 convert_multiply_fusion
  10.0 0.4 mul.57
  10.4 1.5 copy.26
  12.0 0.6 broadcast_in_dim.7
  12.6 2.5 mul.60
  15.1 6.5 %copy.25 = bf16[1024,2048]{0,1:T(8,128)(2,1)} copy(bf16[1024,2048]{1,0:T(8,128)(2,1)} %param.8) | data formatting | bytes 8388608 | tf_op args[2]
  21.7 0.3 add_multiply_fusion
  22.0 4.2 %broadcast_in_dim.8 = f32[1024,4,2,128,2]{0,4,3,2,1:T(2,128)} broadcast(f32[1024,4,128]{0,2,1:T(8,128)S(1)} %bitcast.31), dimensions={0,1,3} | broadcast | bytes 10485760 | tf_op jit(solution)/shard_map/broadcast_in_dim | solution.py:21
  26.2 10.9 %mul.64 = f32[1024,2048]{0,1:T(8,128)} reshape(f32[1024,4,2,128,2]{0,4,3,2,1:T(2,128)} %broadcast_in_dim.8) | data formatting | bytes 16777216 | tf_op jit(solution)/shard_map/mul | solution.py:22
  37.1 37.1 %all-gather.2.cloned.1.call-done = bf16[2048,256]{0,1:T(8,128)(2,1)} async-done(((bf16[2048,32]{0,1:T(8,128)(2,1)}), bf16[2048,256]{0,1:T(8,128)(2,1)}) %all-gather.2.cloned.1.call-update) | async-done | bytes 1048592 | tf_op jit(solution)/shard_map/all_gather | solution.py:42
  74.2 6.6 %fusion.2 = f32[256,1024]{0,1:T(8,128)S(1)} fusion(bf16[2048,256]{0,1:T(8,128)(2,1)} %all-gather.2.cloned.1.call-done, f32[1024,2048]{0,1:T(8,128)} %mul.64, bf16[1024,2048]{0,1:T(8,128)(2,1)} %copy.25), kind=kOutput, calls=%fused_computation.7 | convolution fusion | flops 1080295424 | bytes 14680064 | tf_op jit(solution)/shard_map/dot_general | solution.py:56
  80.9 1.3 copy.32
  82.3 36.4 %all_gather.6 = bf16[1024,256]{0,1:T(8,128)(2,1)S(1)} all-gather(bf16[1024,16]{0,1:T(8,128)(2,1)S(1)} %copy-done.2), channel_id=1, replica_groups=mesh['dp'=2,'pb'=8,'ta'=16] {'ta'}, dimensions={1}, use_global_device_ids=true | all-gather | bytes 557056 | tf_op jit(solution)/shard_map/all_gather | solution.py:41
  118.7 6.1 %fusion.1 = bf16[256,2048]{0,1:T(8,128)(2,1)S(1)} fusion(bf16[1024,256]{0,1:T(8,128)(2,1)S(1)} %all_gather.6, f32[1024,2048]{0,1:T(8,128)} %mul.64, bf16[1024,2048]{0,1:T(8,128)(2,1)} %copy.25), kind=kOutput, calls=%fused_computation.4 | convolution fusion | flops 1081081856 | bytes 14155776 | tf_op jit(solution)/shard_map/dot_general | solution.py:68
  124.8 1.5 copy.34
  126.3 6.1 %fusion.4 = (bf16[1024,2048]{1,0:T(8,128)(2,1)}, f32[1024,2048]{1,0:T(8,128)}) fusion(bf16[1024,256]{0,1:T(8,128)(2,1)S(1)} %all_gather.6, bf16[2048,256]{0,1:T(8,128)(2,1)S(1)} %copy-done.1), kind=kOutput, calls=%fused_computation.16 | convolution fusion | flops 1077936128 | bytes 14155776 | tf_op jit(solution)/shard_map/dot_general | solution.py:34
  132.3 9.3 %copy.23 = f32[1024,2048]{0,1:T(8,128)} copy(f32[1024,2048]{1,0:T(8,128)} %get-tuple-element.29) | data formatting | bytes 16777216 | tf_op jit(solution)/shard_map/mul | solution.py:44
  141.6 10.6 %reshape.58 = f32[1024,4,2,128,2]{0,4,3,2,1:T(2,128)} reshape(f32[1024,2048]{0,1:T(8,128)} %copy.23) | data formatting | bytes 16777216 | tf_op jit(solution)/shard_map/reshape | solution.py:14
  152.2 10.3 %reduce_sum.34 = f32[1024,4,128]{0,2,1:T(8,128)} reduce(f32[1024,4,2,128,2]{0,4,3,2,1:T(2,128)} %reshape.58, f32[]{:T(128)} %constant.4.clone.1), dimensions={2,4}, to_apply=%region_0.0 | reduce | flops 1572864 | bytes 10485764 | tf_op jit(solution)/shard_map/reduce_sum | solution.py:15
  162.5 1.9 broadcast_multiply_fusion
  164.5 2.3 div.24
  166.8 3.1 %reduce_sum.35 = f32[1024,2,64]{0,2,1:T(8,128)S(1)} reduce(f32[1024,2,2,64,2]{0,4,3,2,1:T(2,128)} %div.24, f32[]{:T(128)} %constant.4.clone.1), dimensions={2,4}, to_apply=%region_1.0 | reduce | flops 393216 | bytes 2621444 | tf_op jit(solution)/shard_map/reduce_sum | solution.py:15
  169.8 1.3 copy.31
  171.2 0.1 reduce_sum.37
  171.4 0.3 reduce_sum.38
  171.7 0.8 copy.28
  172.5 0.6 multiply_convert_fusion.1
  173.2 1.0 copy.33
  174.2 0.7 copy.29
  174.9 75.7 %reduce-scatter.9.cloned.1.call-done = bf16[32,2048]{1,0:T(8,128)(2,1)} async-done(((bf16[256,2048]{1,0:T(8,128)(2,1)}), bf16[32,2048]{1,0:T(8,128)(2,1)}) %reduce-scatter.9.cloned.1.call-update) | async-done | bytes 131088
  (15 shorter events, 0.4 us)
Async XLA Ops:
  7.2 67.1 %all-gather.2.cloned.1.call-start = ((), (), s32[]{:S(2)}) async-start(), calls=%async_computation.2 | async-start | bytes 1179648 | tf_op jit(solution)/shard_map/all_gather | solution.py:42
  7.9 165.3 %reduce-scatter.7.cloned.1.call-start = ((), (), s32[]{:S(2)}) async-start(), calls=%async_computation.3 | async-start | bytes 1114112
  15.1 6.5 %copy-start = (f32[1024,512]{0,1:T(8,128)S(1)}, f32[1024,512]{0,1:T(8,128)}, u32[]{:S(2)}) copy-start(f32[1024,512]{0,1:T(8,128)} %mul.60) | copy-start | bytes 6291460
  37.1 45.2 %copy-start.2 = (bf16[1024,16]{0,1:T(8,128)(2,1)S(1)}, bf16[1024,16]{0,1:T(8,128)(2,1)}, u32[]{:S(2)}) copy-start(bf16[1024,16]{0,1:T(8,128)(2,1)} %param.6) | copy-start | bytes 98308
  82.2 168.4 %reduce-scatter.9.cloned.1.call-start = ((), (), s32[]{:S(2)}) async-start(), calls=%async_computation.4 | async-start | bytes 1179648
  118.7 7.5 %copy-start.1 = (bf16[2048,256]{0,1:T(8,128)(2,1)S(1)}, bf16[2048,256]{0,1:T(8,128)(2,1)}, u32[]{:S(2)}) copy-start(bf16[2048,256]{0,1:T(8,128)(2,1)} %all-gather.2.cloned.1.call-done) | copy-start | bytes 3145732
Sparse Core Ops, SparseCore 0:
  10.6 63.5 all-gather.1
  82.3 75.1 reduce-scatter.6
  162.5 88.0 reduce-scatter.8
where the time goes:
time: 260 us; the launch traced here: 257 us
  waiting for transfers between devices  113 us (43%)
  local copies, waits for them, and re-layouts  56.9 us (22%)
  blocking collectives  36.4 us (14%)
  matrix products  18.8 us (7%)
  other arithmetic  17.6 us (7%)
  between operations  13.9 us (5%)
    unnamed x5, waiting for transfers between devices  76.4 us
    all_gather x1, waiting for transfers between devices, body(): target_full = lax.all_gather(fmap2, 'pb', axis=1, tiled=True)  37.1 us
    all_gather x1, blocking collectives, body(): query_full = lax.all_gather(fmap1, 'ta', axis=1, tiled=True)  36.4 us
    unnamed x14, local copies, waits for them, and re-layouts  14.5 us
    reduce_sum x4, other arithmetic, pool_last(): jnp.mean(shaped, axis=(-3, -1)).reshape(lead + (height * across // 4,))  13.8 us
    mul x3, local copies, waits for them, and re-layouts, spread_last(): return 0.25 * shaped.reshape(lead + (height * across * 4,))  13.7 us
    reshape x1, local copies, waits for them, and re-layouts, pool_last(): shaped = volume.reshape(lead + (height // 2, 2, across // 2, 2))  10.6 us
    mul x1, local copies, waits for them, and re-layouts, body(): volume = pair_product(query_full, target_full) * factor  9.28 us
  transfers between devices with their start and end apart: 3, of which 2 were waited for; matrix products, arithmetic and copies ran while one was open for 33% of the time, Pallas kernels for 0%

commit v1 on v0

v1 whole, which is shorter than its diff:
```python
import functools
import math

import jax
import jax.numpy as jnp
from jax import lax
from jax.experimental import pallas as pl
from jax.experimental.pallas import tpu as pltpu
from jax.sharding import PartitionSpec as P

C = 256
W = 256
MESH = pl.DeviceIdType.MESH
BF = jnp.bfloat16
F32 = jnp.float32
FACTOR = 1.0 / math.sqrt(C)


def mm(a, b, ca=1, cb=0):
    return lax.dot_general(a, b, (((ca,), (cb,)), ((), ())), preferred_element_type=F32)


def spread_matrix(rows, shift, value, offset=0):
    row = lax.broadcasted_iota(jnp.int32, (rows, W), 0) - offset
    col = lax.broadcasted_iota(jnp.int32, (rows, W), 1)
    return jnp.where(row == (col >> shift), value, 0.0)


def exchange(
    f1_ref, f2_ref, cot0_ref, cot1_ref, cot2_ref, cot3_ref,
    f1_full, f2_full, gt_sum, gt_in_z, gq_sum, gq_in_z,
    comb, c1, c2, c3, gt, gq, gt_in, gq_in, gt_out, gq_out,
    load_sem, own_sem, f1_send, f1_recv, f2_send, f2_recv, gt_send, gt_recv, gq_send, gq_recv,
):
    dp, pb, ta = lax.axis_index("dp"), lax.axis_index("pb"), lax.axis_index("ta")
    zh, x = pb // 4, pb % 4
    zl, y = ta // 4, ta % 4

    def at_x(k):
        return (dp, zh * 4 + (x + k) % 4, ta)

    def at_y(k):
        return (dp, pb, zl * 4 + (y + k) % 4)

    def at_zl(k):
        return (dp, pb, ((zl + k) % 4) * 4 + y)

    across = (dp, (1 - zh) * 4 + x, ta)

    def copy(src, dst, send, recv, to):
        return pltpu.make_async_remote_copy(
            src_ref=src, dst_ref=dst, send_sem=send, recv_sem=recv, device_id=to, device_id_type=MESH
        )

    loads = [
        pltpu.make_async_copy(src, dst, load_sem.at[i])
        for i, (src, dst) in enumerate(((cot3_ref, c3), (cot2_ref, c2), (cot1_ref, c1), (cot0_ref, comb)))
    ]
    own = [
        pltpu.make_async_copy(f1_ref, f1_full.at[zl, y], own_sem.at[0]),
        pltpu.make_async_copy(f2_ref, f2_full.at[pb], own_sem.at[1]),
    ]
    barrier = pltpu.get_barrier_semaphore()
    peers = [at_x(k) for k in (1, 2, 3)] + [at_y(k) for k in (1, 2, 3)] + [at_zl(k) for k in (1, 2, 3)] + [across]
    for peer in peers:
        pl.semaphore_signal(barrier, inc=1, device_id=peer, device_id_type=MESH)
    for c in own + loads:
        c.start()
    pl.semaphore_wait(barrier, len(peers))

    sent = []
    f1_z, f1_y, f2_x = [], [], []
    for k in (1, 2, 3):
        c = copy(f1_ref, f1_full.at[zl, y], f1_send.at[k - 1], f1_recv.at[k - 1], at_zl(k))
        c.start()
        sent.append(c)
        c = copy(f1_ref, f1_full.at[zl, y], f1_send.at[2 + k], f1_recv.at[2 + k], at_y(k))
        c.start()
        sent.append(c)
    f2_z = copy(f2_ref, f2_full.at[pb], f2_send.at[0], f2_recv.at[0], across)
    f2_z.start()
    sent.append(f2_z)
    for k in (1, 2, 3):
        c = copy(f2_ref, f2_full.at[pb], f2_send.at[k], f2_recv.at[k], at_x(k))
        c.start()
        sent.append(c)

    for k in (1, 2, 3):
        got = f1_full.at[(zl + 4 - k) % 4, y]
        copy(got, got, f1_send.at[k - 1], f1_recv.at[k - 1], at_zl(k)).wait_recv()
        for m in (1, 2, 3):
            i = 3 + 3 * k + m - 1
            c = copy(got, got, f1_send.at[i], f1_recv.at[i], at_y(m))
            c.start()
            sent.append(c)

    own[0].wait()
    own[1].wait()
    a3 = spread_matrix(32, 3, 1.0 / 64).astype(BF)
    fine = spread_matrix(128, 1, 0.25).astype(BF)
    coarse = [spread_matrix(128, 2, 1.0 / 16, 64 * j).astype(BF) for j in range(2)]
    both = [jnp.concatenate([fine, coarse[j]], axis=0) for j in range(2)]
    for c in loads:
        c.wait()

    def merge(i, _):
        rows = pl.ds(pl.multiple_of(i * 256, 256), 256)
        third = mm(c3[:, rows], a3, 0, 0)
        second = c2[rows, :]
        for k in range(4):
            left = jnp.concatenate([c1[rows, k * 128:(k + 1) * 128], second], axis=1)
            upper = mm(left, both[k // 2]) + third
            for r in (2 * k, 2 * k + 1):
                cols = slice(r * W, (r + 1) * W)
                comb[rows, cols] = (comb[rows, cols].astype(F32) + upper).astype(BF)
        return 0

    lax.fori_loop(0, comb.shape[0] // 256, merge, 0)

    other = f2_full.at[(1 - zh) * 4 + x]
    copy(other, other, f2_send.at[0], f2_recv.at[0], across).wait_recv()
    for k in (1, 2, 3):
        c = copy(other, other, f2_send.at[3 + k], f2_recv.at[3 + k], at_x(k))
        c.start()
        sent.append(c)

    for k in (1, 2, 3):
        block = f1_full.at[zl, (y + 4 - k) % 4]
        copy(block, block, f1_send.at[2 + k], f1_recv.at[2 + k], at_y(k)).wait_recv()
        for m in (1, 2, 3):
            i = 3 + 3 * m + k - 1
            block = f1_full.at[(zl + 4 - m) % 4, (y + 4 - k) % 4]
            copy(block, block, f1_send.at[i], f1_recv.at[i], at_y(k)).wait_recv()

    first = f1_full[...].reshape(C, comb.shape[0])

    def target(n, _):
        cols = pl.ds(pl.multiple_of(n * W, W), W)
        part = mm(first, comb[:, cols]) * FACTOR
        gt[:, :, :, cols] = part.astype(BF).reshape(2, 4, 32, W)
        return 0

    lax.fori_loop(0, comb.shape[1] // W, target, 0)
    for h in (0, 1):
        side = (1 - zh) if h == 0 else zh
        for k in (1, 2, 3):
            i = 3 * h + k - 1
            c = copy(gt.at[side, (x + k) % 4], gt_in.at[h, k - 1], gt_send.at[i], gt_recv.at[i], at_x(k))
            c.start()
            sent.append(c)

    for k in (1, 2, 3):
        block = f2_full.at[zh * 4 + (x + 4 - k) % 4]
        copy(block, block, f2_send.at[k], f2_recv.at[k], at_x(k)).wait_recv()
        block = f2_full.at[(1 - zh) * 4 + (x + 4 - k) % 4]
        copy(block, block, f2_send.at[3 + k], f2_recv.at[3 + k], at_x(k)).wait_recv()

    second = f2_full[...].reshape(C, comb.shape[1])

    def query(n, _):
        rows = pl.ds(pl.multiple_of(n * 256, 256), 256)
        part = mm(second, comb[rows, :], 1, 1) * FACTOR
        gq[:, :, :, rows] = part.astype(BF).reshape(4, 4, 16, 256)
        return 0

    lax.fori_loop(0, comb.shape[0] // 256, query, 0)
    for k in (1, 2, 3):
        c = copy(gq.at[:, (y + k) % 4], gq_in.at[k - 1], gq_send.at[k - 1], gq_recv.at[k - 1], at_y(k))
        c.start()
        sent.append(c)

    def gt_total(h, side):
        total = gt[side, x].astype(F32)
        for k in (1, 2, 3):
            i = 3 * h + k - 1
            copy(gt_in.at[h, k - 1], gt_in.at[h, k - 1], gt_send.at[i], gt_recv.at[i], at_x(k)).wait_recv()
            total = total + gt_in[h, k - 1].astype(F32)
        return total

    gt_out[...] = gt_total(0, 1 - zh).astype(BF)
    c = copy(gt_out, gt_in_z, gt_send.at[6], gt_recv.at[6], across)
    c.start()
    sent.append(c)

    for k in (1, 2, 3):
        copy(gq_in.at[k - 1], gq_in.at[k - 1], gq_send.at[k - 1], gq_recv.at[k - 1], at_y(k)).wait_recv()
    for k in (1, 2, 3, 0):
        to = (zl + k) % 4
        total = gq[to, y].astype(F32)
        for m in range(3):
            total = total + gq_in[m, to].astype(F32)
        if k:
            gq_out[k - 1] = total.astype(BF)
            c = copy(gq_out.at[k - 1], gq_in_z.at[k - 1], gq_send.at[2 + k], gq_recv.at[2 + k], at_zl(k))
            c.start()
            sent.append(c)
        else:
            gq_sum[...] = total
    gt_sum[...] = gt_total(1, zh)

    for k in (1, 2, 3):
        copy(gq_in_z.at[k - 1], gq_in_z.at[k - 1], gq_send.at[2 + k], gq_recv.at[2 + k], at_zl(k)).wait_recv()
    copy(gt_in_z, gt_in_z, gt_send.at[6], gt_recv.at[6], across).wait_recv()
    for c in sent:
        c.wait_send()


def volumes(
    f1_ref, f2_ref, gt_sum, gt_in_z, gq_sum, gq_in_z,
    corr0, corr1, corr2, corr3, grad_query, grad_target,
    p1, p2, p3,
):
    @pl.when(pl.program_id(0) == 0)
    def _():
        grad_target[...] = (gt_sum[...] + gt_in_z[...].astype(F32)).astype(BF)
        total = gq_sum[...]
        for k in range(3):
            total = total + gq_in_z[k].astype(F32)
        grad_query[...] = total.astype(BF)
        narrow = [spread_matrix(W // 2 ** l, l, 4.0 ** -l).astype(BF) for l in (1, 2, 3)]
        mean = jnp.concatenate(narrow + [jnp.zeros((32, W), BF)], axis=0)
        rows = [mm(f2_ref[:, r * W:(r + 1) * W], mean, 1, 1) for r in range(8)]
        pairs = [rows[2 * k] + rows[2 * k + 1] for k in range(4)]
        fours = [pairs[2 * k] + pairs[2 * k + 1] for k in range(2)]
        eight = fours[0] + fours[1]

        def put(ref, value, cols):
            high = value.astype(BF)
            ref[0, :, cols] = high
            ref[1, :, cols] = (value - high.astype(F32)).astype(BF)

        for k in range(4):
            put(p1, pairs[k][:, :128], slice(k * 128, (k + 1) * 128))
        put(p2, jnp.concatenate([f[:, 128:192] for f in fours], axis=1), slice(0, 128))
        put(p3, eight[:, 192:224], slice(0, 32))

    columns = f1_ref[...]
    query = columns.T
    corr0[...] = (mm(query, f2_ref[...]) * FACTOR).astype(BF)
    corr1[...] = ((mm(query, p1[0]) + mm(query, p1[1])) * FACTOR).astype(BF)
    corr2[...] = ((mm(query, p2[0]) + mm(query, p2[1])) * FACTOR).astype(BF)
    corr3[...] = ((mm(p3[0], columns, 0, 0) + mm(p3[1], columns, 0, 0)) * FACTOR).astype(BF)


def body(fmap1, fmap2, cot0, cot1, cot2, cot3):
    nq, nt = cot0.shape
    hbm = pl.BlockSpec(memory_space=pltpu.HBM)
    vmem = pl.BlockSpec(memory_space=pltpu.VMEM)
    dma = pltpu.SemaphoreType.DMA
    sds = jax.ShapeDtypeStruct
    f1_full, f2_full, gt_sum, gt_in_z, gq_sum, gq_in_z = pl.pallas_call(
        exchange,
        out_shape=(
            sds((4, 4, 16, nq), BF),
            sds((8, 32, nt), BF),
            sds((32, nt), F32),
            sds((32, nt), BF),
            sds((16, nq), F32),
            sds((3, 16, nq), BF),
        ),
        in_specs=[hbm] * 6,
        out_specs=(vmem,) * 6,
        scratch_shapes=[
            pltpu.VMEM((nq, nt), BF),
            pltpu.VMEM((nq, nt // 4), BF),
            pltpu.VMEM((nq, nt // 16), BF),
            pltpu.VMEM((nt // 64, nq), BF),
            pltpu.VMEM((2, 4, 32, nt), BF),
            pltpu.VMEM((4, 4, 16, nq), BF),
            pltpu.VMEM((2, 3, 32, nt), BF),
            pltpu.VMEM((3, 4, 16, nq), BF),
            pltpu.VMEM((32, nt), BF),
            pltpu.VMEM((3, 16, nq), BF),
            dma((4,)),
            dma((2,)),
            dma((15,)),
            dma((15,)),
            dma((7,)),
            dma((7,)),
            dma((7,)),
            dma((7,)),
            dma((6,)),
            dma((6,)),
        ],
        compiler_params=pltpu.CompilerParams(
            collective_id=0, has_side_effects=True, vmem_limit_bytes=40 * 2**20
        ),
        cost_estimate=pl.CostEstimate(flops=6 * nq * nt * C, bytes_accessed=16 * 2**20, transcendentals=0),
        name="exchange",
    )(*(pltpu.with_memory_space_constraint(a, pltpu.HBM) for a in (fmap1.T, fmap2.T, cot0, cot1, cot2, cot3.T)))

    block = 128
    whole = lambda *shape: pl.BlockSpec(shape, lambda i: (0,) * len(shape))
    corr0, corr1, corr2, corr3, grad_query, grad_target = pl.pallas_call(
        volumes,
        grid=(nq // block,),
        out_shape=(
            sds((nq, nt), BF),
            sds((nq, nt // 4), BF),
            sds((nq, nt // 16), BF),
            sds((nt // 64, nq), BF),
            sds((16, nq), BF),
            sds((32, nt), BF),
        ),
        in_specs=[
            pl.BlockSpec((C, block), lambda i: (0, i)),
            whole(C, nt),
            whole(32, nt),
            whole(32, nt),
            whole(16, nq),
            whole(3, 16, nq),
        ],
        out_specs=(
            pl.BlockSpec((block, nt), lambda i: (i, 0)),
            pl.BlockSpec((block, nt // 4), lambda i: (i, 0)),
            pl.BlockSpec((block, nt // 16), lambda i: (i, 0)),
            pl.BlockSpec((nt // 64, block), lambda i: (0, i)),
            whole(16, nq),
            whole(32, nt),
        ),
        scratch_shapes=[
            pltpu.VMEM((2, C, nt // 4), BF),
            pltpu.VMEM((2, C, nt // 16), BF),
            pltpu.VMEM((2, C, nt // 64), BF),
        ],
        compiler_params=pltpu.CompilerParams(vmem_limit_bytes=40 * 2**20),
        cost_estimate=pl.CostEstimate(flops=4 * nq * nt * C, bytes_accessed=8 * 2**20, transcendentals=0),
        name="volumes",
    )(f1_full.reshape(C, nq), f2_full.reshape(C, nt), gt_sum, gt_in_z, gq_sum, gq_in_z)
    return corr0, corr1, corr2, corr3.T, grad_query.T, grad_target.T


def solution(mesh):
    rows, flat = P(("dp", "pb"), "ta"), P(("dp", "ta"), "pb")
    return jax.shard_map(
        body,
        mesh=mesh,
        in_specs=(rows, flat, rows, rows, rows, rows),
        out_specs=(rows, rows, rows, rows, rows, flat),
        check_vma=False,
    )
```

time: 260 us -> 50.4 us (0.19)
  waiting for transfers between devices: 113 us -> 0 us
  local copies, waits for them, and re-layouts: 56.9 us -> 0 us
  Pallas kernels: 0 us -> 49.3 us
  blocking collectives: 36.4 us -> 0 us
  matrix products: 18.8 us -> 0 us
  other arithmetic: 17.6 us -> 0 us
  between operations: 13.9 us -> 0.64 us
    unnamed x5 -> x0, waiting for transfers between devices: 76.4 us -> none
    pallas_call x0 -> x2, Pallas kernels: none -> 49.3 us  [the longest x1 43.3 us: body(): pl.pallas_call(exchange, out_shape=(sds((4, 4, 16, nq), BF), sds((8, 32,...]
    all_gather x1 -> x0, waiting for transfers between devices: 37.1 us -> none  [body(): target_full = lax.all_gather(fmap2, 'pb', axis=1, tiled=True)]
    all_gather x1 -> x0, blocking collectives: 36.4 us -> none  [body(): query_full = lax.all_gather(fmap1, 'ta', axis=1, tiled=True)]
    mul x4 -> x0, local copies, waits for them, and re-layouts: 23 us -> none  [the longest x3 13.7 us: spread_last(): return 0.25 * shaped.reshape(lead + (height * across * 4,))]
    dot_general x3 -> x0, matrix products: 18.8 us -> none  [the longest x1 6.64 us: body(): lax.dot_general(channel, weights, (((0,), (1,)), ((), ())), preferred_ele...]
    unnamed x14 -> x0, local copies, waits for them, and re-layouts: 14.5 us -> none
    reduce_sum x4 -> x0, other arithmetic: 13.8 us -> none  [pool_last(): jnp.mean(shaped, axis=(-3, -1)).reshape(lead + (height * across // 4,))]
  transfers between devices with their start and end apart: 3 -> 0, of which waited for: 2 -> 0; matrix products, arithmetic and copies ran while one was open for 33% -> 0% of each run, Pallas kernels for 0% -> 0%
where the time goes in v1:
time: 50.4 us; the launch traced here: 49.9 us
  Pallas kernels  49.3 us (98%)
  between operations  0.64 us (1%)
    pallas_call x1, Pallas kernels, body(): pl.pallas_call(exchange, out_shape=(sds((4, 4, 16, nq), BF), sds((8, 32,...  43.3 us
    pallas_call x1, Pallas kernels, body(): pl.pallas_call(volumes, grid=(nq // block,), out_shape=(sds((nq, nt), BF)...  5.92 us

profile of v1, /device:TPU:32, one launch (start us, length us, event | category | flops | bytes accessed | tf_op | source)
XLA Modules:
  0.0 49.9 jit_solution(5803390966221259901)
XLA Ops:
  0.6 43.3 %exchange.1 = (bf16[4,4,16,1024]{3,2,1,0:T(8,128)(2,1)S(1)}, bf16[8,32,2048]{2,1,0:T(8,128)(2,1)S(1)}, f32[32,2048]{1,0:T(8,128)S(1)}, bf16[32,2048]{1,0:T(8,128...) custom-call(bf16[16,1024]{1,0:T(8,128)(2,1)} %bitcast.12, bf16[32,2048]{1,0:T(8,128)(2,1)} %bitcast.10, ...), custom_call_target="tpu_custom_call" | custom-call | flops 3221225472 | bytes 16777216 | tf_op jit(solution)/shard_map/exchange/pallas_call | solution.py:251
  44.0 5.9 %volumes.1 = (bf16[1024,2048]{1,0:T(8,128)(2,1)}, bf16[1024,512]{1,0:T(8,128)(2,1)}, bf16[1024,128]{1,0:T(8,128)(2,1)}, bf16[32,1024]{1,0:T(8,128)(2,1)}, bf16[1...) custom-call(bf16[256,1024]{1,0:T(8,128)(2,1)S(1)} %bitcast.9, bf16[256,2048]{1,0:T(8,128)(2,1)S(1)} %bitcast.8, ...), custom_call_target="tpu_custom_call" | custom-call | flops 2147483648 | bytes 8388608 | tf_op jit(solution)/shard_map/volumes/pallas_call | solution.py:294

commit v2 on v1

v2 whole, which is shorter than its diff:
```python
import functools
import math

import jax
import jax.numpy as jnp
from jax import lax
from jax.experimental import pallas as pl
from jax.experimental.pallas import tpu as pltpu
from jax.sharding import PartitionSpec as P

C = 256
W = 256
MESH = pl.DeviceIdType.MESH
BF = jnp.bfloat16
F32 = jnp.float32
FACTOR = 1.0 / math.sqrt(C)


def mm(a, b, ca=1, cb=0):
    return lax.dot_general(a, b, (((ca,), (cb,)), ((), ())), preferred_element_type=F32)


def spread_matrix(rows, shift, value, offset=0):
    row = lax.broadcasted_iota(jnp.int32, (rows, W), 0) - offset
    col = lax.broadcasted_iota(jnp.int32, (rows, W), 1)
    return jnp.where(row == (col >> shift), value, 0.0)


def exchange(
    f1_ref, f2_ref, cot0_ref, cot1_ref, cot2_ref, cot3_ref,
    corr0, corr1, corr2, corr3, gt_sum, gt_in_z, gq_sum, gq_in_z,
    f1_full, f2_full, comb, c1, c2, c3, p1, p2, p3, gt, gq, gt_in, gt_mid, gt_out, gq_in, gq_out,
    load_sem, own_sem, f1_send, f1_recv, f2_send, f2_recv, gt_send, gt_recv, gq_send, gq_recv,
):
    dp, pb, ta = lax.axis_index("dp"), lax.axis_index("pb"), lax.axis_index("ta")
    zh, x = pb // 4, pb % 4
    zl, y = ta // 4, ta % 4
    nq, nt = comb.shape
    halves = (pl.ds(0, 16), pl.ds(16, 16))

    def near(k):
        return (x + k) % 4

    def at_x(k):
        return (dp, zh * 4 + near(k), ta)

    def at_y(k):
        return (dp, pb, zl * 4 + (y + k) % 4)

    def at_zl(k):
        return (dp, pb, ((zl + k) % 4) * 4 + y)

    across = (dp, (1 - zh) * 4 + x, ta)

    def copy(src, dst, send, recv, to):
        return pltpu.make_async_remote_copy(
            src_ref=src, dst_ref=dst, send_sem=send, recv_sem=recv, device_id=to, device_id_type=MESH
        )

    sent = []

    def start(*args):
        c = copy(*args)
        c.start()
        sent.append(c)

    def arrived(dst, send, recv, to):
        copy(dst, dst, send, recv, to).wait_recv()

    loads = [
        pltpu.make_async_copy(src, dst, load_sem.at[i])
        for i, (src, dst) in enumerate(((cot3_ref, c3), (cot2_ref, c2), (cot1_ref, c1), (cot0_ref, comb)))
    ]
    own = [
        pltpu.make_async_copy(f1_ref, f1_full.at[zl, y], own_sem.at[0]),
        pltpu.make_async_copy(f2_ref, f2_full.at[pb], own_sem.at[1]),
    ]
    barrier = pltpu.get_barrier_semaphore()
    peers = [at_x(k) for k in (1, 3)] + [at_y(k) for k in (1, 2, 3)] + [at_zl(k) for k in (1, 2, 3)] + [across]
    for peer in peers:
        pl.semaphore_signal(barrier, inc=1, device_id=peer, device_id_type=MESH)
    for c in own + loads:
        c.start()
    pl.semaphore_wait(barrier, len(peers))

    def ring_first(side, src, part):
        h = 0 if side is None else 1
        base = 2 + 6 * h
        block = f2_full.at[pb if h == 0 else (1 - zh) * 4 + x, halves[part]]
        for way, k in ((0, 1), (1, 3)):
            i = base + way + (0 if part == way else 2)
            start(src, block, f2_send.at[i], f2_recv.at[i], at_x(k))

    def block_of(h, k):
        return (zh if h == 0 else 1 - zh) * 4 + near(k)

    def ring_second(h, way):
        base = 2 + 6 * h
        back, on = ((3, 1), (1, 3))[way]
        got = f2_full.at[block_of(h, back), halves[way]]
        arrived(got, f2_send.at[base + way], f2_recv.at[base + way], at_x(on))
        start(got, got, f2_send.at[base + 4 + way], f2_recv.at[base + 4 + way], at_x(on))

    def ring_rest(h):
        base = 2 + 6 * h
        for way, (back, on) in enumerate(((3, 1), (1, 3))):
            got = f2_full.at[block_of(h, back), halves[1 - way]]
            arrived(got, f2_send.at[base + 2 + way], f2_recv.at[base + 2 + way], at_x(on))
            got = f2_full.at[block_of(h, 2), halves[way]]
            arrived(got, f2_send.at[base + 4 + way], f2_recv.at[base + 4 + way], at_x(on))

    for k in (1, 2, 3):
        start(f1_ref, f1_full.at[zl, y], f1_send.at[k - 1], f1_recv.at[k - 1], at_zl(k))
    for part in (0, 1):
        start(
            f2_ref.at[halves[part]], f2_full.at[pb, halves[part]], f2_send.at[part], f2_recv.at[part], across
        )
    for part in (0, 1):
        ring_first(None, f2_ref.at[halves[part]], part)
    for k in (1, 2, 3):
        start(f1_ref, f1_full.at[zl, y], f1_send.at[2 + k], f1_recv.at[2 + k], at_y(k))

    a3 = spread_matrix(32, 3, 1.0 / 64).astype(BF)
    fine = spread_matrix(128, 1, 0.25).astype(BF)
    coarse = [spread_matrix(128, 2, 1.0 / 16, 64 * j).astype(BF) for j in range(2)]
    both = [jnp.concatenate([fine, coarse[j]], axis=0) for j in range(2)]
    ring_second(0, 0)
    ring_second(0, 1)

    for k in (1, 2, 3):
        got = f1_full.at[(zl + 4 - k) % 4, y]
        arrived(got, f1_send.at[k - 1], f1_recv.at[k - 1], at_zl(k))
        for m in (1, 2, 3):
            i = 3 + 3 * k + m - 1
            start(got, got, f1_send.at[i], f1_recv.at[i], at_y(m))

    for c in own + loads:
        c.wait()

    def merge(i, _):
        rows = pl.ds(pl.multiple_of(i * 256, 256), 256)
        third = mm(c3[:, rows], a3, 0, 0)
        second = c2[rows, :]
        for k in range(4):
            left = jnp.concatenate([c1[rows, k * 128:(k + 1) * 128], second], axis=1)
            upper = mm(left, both[k // 2]) + third
            for r in (2 * k, 2 * k + 1):
                cols = slice(r * W, (r + 1) * W)
                comb[rows, cols] = (comb[rows, cols].astype(F32) + upper).astype(BF)
        return 0

    def other_first(part):
        got = f2_full.at[(1 - zh) * 4 + x, halves[part]]
        arrived(got, f2_send.at[part], f2_recv.at[part], across)
        ring_first(1, got, part)

    steps = nq // 256
    lax.fori_loop(0, steps // 2, merge, 0)
    other_first(0)
    other_first(1)
    lax.fori_loop(steps // 2, steps, merge, 0)

    for k in (1, 2, 3):
        arrived(f1_full.at[zl, (y + 4 - k) % 4], f1_send.at[2 + k], f1_recv.at[2 + k], at_y(k))
        for m in (1, 2, 3):
            i = 3 + 3 * m + k - 1
            arrived(f1_full.at[(zl + 4 - m) % 4, (y + 4 - k) % 4], f1_send.at[i], f1_recv.at[i], at_y(k))
    ring_second(1, 0)
    ring_second(1, 1)

    first = f1_full[...].reshape(C, nq)

    def target(n, _):
        cols = pl.ds(pl.multiple_of(n * W, W), W)
        part = mm(first, comb[:, cols]) * FACTOR
        gt[:, :, :, cols] = part.astype(BF).reshape(2, 4, 32, W)
        return 0

    lax.fori_loop(0, nt // W, target, 0)

    def side_of(h):
        return (1 - zh) if h == 0 else zh

    def scatter_first(h):
        base = 6 * h
        for way, k in ((0, 1), (1, 3)):
            start(
                gt.at[side_of(h), near(2), halves[way]], gt_in.at[h, way],
                gt_send.at[base + way], gt_recv.at[base + way], at_x(k),
            )
        for way, k in ((0, 1), (1, 3)):
            start(
                gt.at[side_of(h), near(k), halves[1 - way]], gt_in.at[h, 2 + way],
                gt_send.at[base + 2 + way], gt_recv.at[base + 2 + way], at_x(k),
            )

    def scatter_second(h):
        base = 6 * h
        for way, k in ((0, 1), (1, 3)):
            arrived(gt_in.at[h, way], gt_send.at[base + way], gt_recv.at[base + way], at_x(k))
            here = gt[side_of(h), near(k), halves[way], :].astype(F32)
            gt_mid[h, way] = (here + gt_in[h, way].astype(F32)).astype(BF)
            start(
                gt_mid.at[h, way], gt_in.at[h, 4 + way],
                gt_send.at[base + 4 + way], gt_recv.at[base + 4 + way], at_x(k),
            )

    def scatter_total(h, part):
        base = 6 * h
        total = gt[side_of(h), x, halves[part], :].astype(F32)
        for way, k in ((0, 1), (1, 3)):
            i = (4 if way == part else 2) + way
            arrived(gt_in.at[h, i], gt_send.at[base + i], gt_recv.at[base + i], at_x(k))
            total = total + gt_in[h, i].astype(F32)
        return total

    scatter_first(0)
    scatter_first(1)

    ring_rest(0)
    ring_rest(1)

    second = f2_full[...].reshape(C, nt)

    def query(n, _):
        rows = pl.ds(pl.multiple_of(n * 256, 256), 256)
        part = mm(second, comb[rows, :], 1, 1) * FACTOR
        gq[:, :, :, rows] = part.astype(BF).reshape(4, 4, 16, 256)
        return 0

    lax.fori_loop(0, nq // 256, query, 0)
    for k in (1, 2, 3):
        start(gq.at[:, (y + k) % 4], gq_in.at[k - 1], gq_send.at[k - 1], gq_recv.at[k - 1], at_y(k))

    scatter_second(0)
    scatter_second(1)

    narrow = [spread_matrix(W // 2 ** l, l, 4.0 ** -l).astype(BF) for l in (1, 2, 3)]
    mean = jnp.concatenate(narrow + [jnp.zeros((32, W), BF)], axis=0)
    images = [mm(second[:, r * W:(r + 1) * W], mean, 1, 1) for r in range(8)]
    pairs = [images[2 * k] + images[2 * k + 1] for k in range(4)]
    fours = [pairs[2 * k] + pairs[2 * k + 1] for k in range(2)]
    eight = fours[0] + fours[1]

    def put(ref, value, cols):
        high = value.astype(BF)
        ref[0, :, cols] = high
        ref[1, :, cols] = (value - high.astype(F32)).astype(BF)

    for k in range(4):
        put(p1, pairs[k][:, :128], slice(k * 128, (k + 1) * 128))
    put(p2, jnp.concatenate([f[:, 128:192] for f in fours], axis=1), slice(0, 128))
    put(p3, eight[:, 192:224], slice(0, 32))

    def volume(n, _):
        rows = pl.ds(pl.multiple_of(n * 256, 256), 256)
        columns = f1_full[:, :, :, rows].reshape(C, 256)
        query = columns.T
        for r in range(8):
            cols = slice(r * W, (r + 1) * W)
            corr0[rows, cols] = (mm(query, f2_full[:, :, cols].reshape(C, W)) * FACTOR).astype(BF)
        corr1[rows, :] = ((mm(query, p1[0]) + mm(query, p1[1])) * FACTOR).astype(BF)
        corr2[rows, :] = ((mm(query, p2[0]) + mm(query, p2[1])) * FACTOR).astype(BF)
        corr3[:, rows] = ((mm(p3[0], columns, 0, 0) + mm(p3[1], columns, 0, 0)) * FACTOR).astype(BF)
        return 0

    lax.fori_loop(0, nq // 256, volume, 0)

    for part in (0, 1):
        gt_out[halves[part], :] = scatter_total(0, part).astype(BF)
        start(
            gt_out.at[halves[part]], gt_in_z.at[halves[part]], gt_send.at[12 + part], gt_recv.at[12 + part], across
        )

    for k in (1, 2, 3):
        arrived(gq_in.at[k - 1], gq_send.at[k - 1], gq_recv.at[k - 1], at_y(k))
    for k in (1, 2, 3, 0):
        to = (zl + k) % 4
        total = gq[to, y].astype(F32)
        for m in range(3):
            total = total + gq_in[m, to].astype(F32)
        if k:
            gq_out[k - 1] = total.astype(BF)
            start(gq_out.at[k - 1], gq_in_z.at[k - 1], gq_send.at[2 + k], gq_recv.at[2 + k], at_zl(k))
        else:
            gq_sum[...] = total
    for part in (0, 1):
        gt_sum[halves[part], :] = scatter_total(1, part)

    for k in (1, 2, 3):
        arrived(gq_in_z.at[k - 1], gq_send.at[2 + k], gq_recv.at[2 + k], at_zl(k))
    for part in (0, 1):
        arrived(gt_in_z.at[halves[part]], gt_send.at[12 + part], gt_recv.at[12 + part], across)
    for c in sent:
        c.wait_send()


def finish(
    v0, v1, v2, v3, gt_sum, gt_in_z, gq_sum, gq_in_z,
    corr0, corr1, corr2, corr3, grad_query, grad_target,
    gq, gt, sem,
):
    copies = [
        pltpu.make_async_copy(src, dst, sem.at[i])
        for i, (src, dst) in enumerate(
            ((v0, corr0), (v1, corr1), (v2, corr2), (v3, corr3), (gq, grad_query), (gt, grad_target))
        )
    ]
    for c in copies[:4]:
        c.start()
    total = gq_sum[...]
    for k in range(3):
        total = total + gq_in_z[k].astype(F32)
    gq[...] = total.astype(BF)
    copies[4].start()
    gt[...] = (gt_sum[...] + gt_in_z[...].astype(F32)).astype(BF)
    copies[5].start()
    for c in copies:
        c.wait()


def body(fmap1, fmap2, cot0, cot1, cot2, cot3):
    nq, nt = cot0.shape
    hbm = pl.BlockSpec(memory_space=pltpu.HBM)
    vmem = pl.BlockSpec(memory_space=pltpu.VMEM)
    dma = pltpu.SemaphoreType.DMA
    sds = jax.ShapeDtypeStruct
    volumes = (sds((nq, nt), BF), sds((nq, nt // 4), BF), sds((nq, nt // 16), BF), sds((nt // 64, nq), BF))
    args = (fmap1.T, fmap2.T, cot0, cot1, cot2, cot3.T)
    parts = pl.pallas_call(
        exchange,
        out_shape=volumes + (
            sds((32, nt), F32),
            sds((32, nt), BF),
            sds((16, nq), F32),
            sds((3, 16, nq), BF),
        ),
        in_specs=[hbm] * 6,
        out_specs=(vmem,) * 8,
        scratch_shapes=[
            pltpu.VMEM((4, 4, 16, nq), BF),
            pltpu.VMEM((8, 32, nt), BF),
            pltpu.VMEM((nq, nt), BF),
            pltpu.VMEM((nq, nt // 4), BF),
            pltpu.VMEM((nq, nt // 16), BF),
            pltpu.VMEM((nt // 64, nq), BF),
            pltpu.VMEM((2, C, nt // 4), BF),
            pltpu.VMEM((2, C, nt // 16), BF),
            pltpu.VMEM((2, C, nt // 64), BF),
            pltpu.VMEM((2, 4, 32, nt), BF),
            pltpu.VMEM((4, 4, 16, nq), BF),
            pltpu.VMEM((2, 6, 16, nt), BF),
            pltpu.VMEM((2, 2, 16, nt), BF),
            pltpu.VMEM((32, nt), BF),
            pltpu.VMEM((3, 4, 16, nq), BF),
            pltpu.VMEM((3, 16, nq), BF),
            dma((4,)),
            dma((2,)),
            dma((15,)),
            dma((15,)),
            dma((14,)),
            dma((14,)),
            dma((14,)),
            dma((14,)),
            dma((6,)),
            dma((6,)),
        ],
        compiler_params=pltpu.CompilerParams(
            collective_id=0, has_side_effects=True, vmem_limit_bytes=40 * 2**20
        ),
        cost_estimate=pl.CostEstimate(flops=10 * nq * nt * C, bytes_accessed=16 * 2**20, transcendentals=0),
        name="exchange",
    )(*(pltpu.with_memory_space_constraint(a, pltpu.HBM) for a in args))
    corr0, corr1, corr2, corr3, grad_query, grad_target = pl.pallas_call(
        finish,
        out_shape=volumes + (sds((16, nq), BF), sds((32, nt), BF)),
        in_specs=[vmem] * 8,
        out_specs=(hbm,) * 6,
        scratch_shapes=[pltpu.VMEM((16, nq), BF), pltpu.VMEM((32, nt), BF), dma((6,))],
        compiler_params=pltpu.CompilerParams(vmem_limit_bytes=16 * 2**20),
        cost_estimate=pl.CostEstimate(flops=0, bytes_accessed=8 * 2**20, transcendentals=0),
        name="finish",
    )(*parts)
    return corr0, corr1, corr2, corr3.T, grad_query.T, grad_target.T


def solution(mesh):
    rows, flat = P(("dp", "pb"), "ta"), P(("dp", "ta"), "pb")
    return jax.shard_map(
        body,
        mesh=mesh,
        in_specs=(rows, flat, rows, rows, rows, rows),
        out_specs=(rows, rows, rows, rows, rows, flat),
        check_vma=False,
    )
```

time: 50.4 us -> 47.1 us (0.935)
  Pallas kernels: 49.3 us -> 46.4 us
    pallas_call x2, Pallas kernels: 49.3 us -> 46.4 us  [the longest x1 43.9 us: body(): pl.pallas_call(exchange, out_shape=volumes + (sds((32, nt), F32), sds((32...]
where the time goes in v2:
time: 47.1 us; the launch traced here: 47 us
  Pallas kernels  46.4 us (99%)
  between operations  0.64 us (1%)
    pallas_call x1, Pallas kernels, body(): pl.pallas_call(exchange, out_shape=volumes + (sds((32, nt), F32), sds((32...  43.9 us
    pallas_call x1, Pallas kernels, body(): pl.pallas_call(finish, out_shape=volumes + (sds((16, nq), BF), sds((32, n...  2.52 us

profile of v2, /device:TPU:32, one launch (start us, length us, event | category | flops | bytes accessed | tf_op | source)
XLA Modules:
  0.0 47.0 jit_solution(5344483177613998889)
XLA Ops:
  0.6 43.9 %exchange.1 = (bf16[1024,2048]{1,0:T(8,128)(2,1)S(1)}, bf16[1024,512]{1,0:T(8,128)(2,1)S(1)}, bf16[1024,128]{1,0:T(8,128)(2,1)S(1)}, bf16[32,1024]{1,0:T(8,128)(...) custom-call(bf16[16,1024]{1,0:T(8,128)(2,1)} %bitcast.10, ...), custom_call_target="tpu_custom_call" | custom-call | flops 5368709120 | bytes 16777216 | tf_op jit(solution)/shard_map/exchange/pallas_call | solution.py:330
  44.5 2.5 %finish.1 = (bf16[1024,2048]{1,0:T(8,128)(2,1)}, bf16[1024,512]{1,0:T(8,128)(2,1)}, bf16[1024,128]{1,0:T(8,128)(2,1)}, bf16[32,1024]{1,0:T(8,128)(2,1)}, bf16[16...) custom-call(bf16[1024,2048]{1,0:T(8,128)(2,1)S(1)} %get-tuple-element.20.v0, bf16[1024,512]{1,0:T(8,128)(2,1)S(1)} %get-tuple-element.21.v1, ...), custom_call_target="tpu_custom_call" | custom-call | bytes 8388608 | tf_op jit(solution)/shard_map/finish/pallas_call | solution.py:374

commit v3 on v2

--- a/solution.py
+++ b/solution.py
@@ -29,7 +29,7 @@
 def exchange(
     f1_ref, f2_ref, cot0_ref, cot1_ref, cot2_ref, cot3_ref,
     corr0, corr1, corr2, corr3, gt_sum, gt_in_z, gq_sum, gq_in_z,
-    f1_full, f2_full, comb, c1, c2, c3, p1, p2, p3, gt, gq, gt_in, gt_mid, gt_out, gq_in, gq_out,
+    f1_full, f2_full, comb, c1, c2, c3, p1, p2, p3, gt, gq, gt_in, gt_out, gq_in, gq_out,
     load_sem, own_sem, f1_send, f1_recv, f2_send, f2_recv, gt_send, gt_recv, gq_send, gq_recv,
 ):
     dp, pb, ta = lax.axis_index("dp"), lax.axis_index("pb"), lax.axis_index("ta")
@@ -76,47 +76,63 @@
         pltpu.make_async_copy(f2_ref, f2_full.at[pb], own_sem.at[1]),
     ]
     barrier = pltpu.get_barrier_semaphore()
-    peers = [at_x(k) for k in (1, 3)] + [at_y(k) for k in (1, 2, 3)] + [at_zl(k) for k in (1, 2, 3)] + [across]
+    peers = [at_x(k) for k in (1, 2, 3)] + [at_y(k) for k in (1, 2, 3)] + [at_zl(k) for k in (1, 2, 3)] + [across]
     for peer in peers:
         pl.semaphore_signal(barrier, inc=1, device_id=peer, device_id_type=MESH)
     for c in own + loads:
         c.start()
     pl.semaphore_wait(barrier, len(peers))
 
-    def ring_first(side, src, part):
-        h = 0 if side is None else 1
-        base = 2 + 6 * h
-        block = f2_full.at[pb if h == 0 else (1 - zh) * 4 + x, halves[part]]
+    def ring_first(part):
         for way, k in ((0, 1), (1, 3)):
-            i = base + way + (0 if part == way else 2)
-            start(src, block, f2_send.at[i], f2_recv.at[i], at_x(k))
-
-    def block_of(h, k):
-        return (zh if h == 0 else 1 - zh) * 4 + near(k)
-
-    def ring_second(h, way):
-        base = 2 + 6 * h
+            i = way + (0 if part == way else 2)
+            start(f2_ref.at[halves[part]], f2_full.at[pb, halves[part]], f2_send.at[i], f2_recv.at[i], at_x(k))
+
+    def ring_second(way):
         back, on = ((3, 1), (1, 3))[way]
-        got = f2_full.at[block_of(h, back), halves[way]]
-        arrived(got, f2_send.at[base + way], f2_recv.at[base + way], at_x(on))
-        start(got, got, f2_send.at[base + 4 + way], f2_recv.at[base + 4 + way], at_x(on))
-
-    def ring_rest(h):
-        base = 2 + 6 * h
+        got = f2_full.at[zh * 4 + near(back), halves[way]]
+        arrived(got, f2_send.at[way], f2_recv.at[way], at_x(on))
+        start(got, got, f2_send.at[4 + way], f2_recv.at[4 + way], at_x(on))
+
+    def ring_rest():
         for way, (back, on) in enumerate(((3, 1), (1, 3))):
-            got = f2_full.at[block_of(h, back), halves[1 - way]]
-            arrived(got, f2_send.at[base + 2 + way], f2_recv.at[base + 2 + way], at_x(on))
-            got = f2_full.at[block_of(h, 2), halves[way]]
-            arrived(got, f2_send.at[base + 4 + way], f2_recv.at[base + 4 + way], at_x(on))
+            got = f2_full.at[zh * 4 + near(back), halves[1 - way]]
+            arrived(got, f2_send.at[2 + way], f2_recv.at[2 + way], at_x(on))
+            got = f2_full.at[zh * 4 + near(2), halves[way]]
+            arrived(got, f2_send.at[4 + way], f2_recv.at[4 + way], at_x(on))
+
+    pieces = [pl.ds(c * (nt // 4), nt // 4) for c in range(4)]
+    piece_copies = [
+        copy(
+            f2_ref.at[:, pieces[c]], f2_full.at[pb, :, pieces[c]], f2_send.at[6 + c], f2_recv.at[6 + c], across
+        )
+        for c in range(4)
+    ]
+
+    def next_piece(c):
+        piece_copies[c - 1].wait_send()
+        piece_copies[c].start()
+
+    def pass_piece(c):
+        got = f2_full.at[(1 - zh) * 4 + x, :, pieces[c]]
+        arrived(got, f2_send.at[6 + c], f2_recv.at[6 + c], across)
+        for k in (1, 2, 3):
+            i = 9 + 3 * c + k
+            start(got, got, f2_send.at[i], f2_recv.at[i], at_x(k))
+
+    def await_pieces():
+        for c in range(4):
+            for k in (1, 2, 3):
+                i = 9 + 3 * c + k
+                arrived(f2_full.at[(1 - zh) * 4 + near(4 - k), :, pieces[c]], f2_send.at[i], f2_recv.at[i], at_x(k))
 
     for k in (1, 2, 3):
         start(f1_ref, f1_full.at[zl, y], f1_send.at[k - 1], f1_recv.at[k - 1], at_zl(k))
+    for c in piece_copies:
+        c.start()
+        sent.append(c)
     for part in (0, 1):
-        start(
-            f2_ref.at[halves[part]], f2_full.at[pb, halves[part]], f2_send.at[part], f2_recv.at[part], across
-        )
-    for part in (0, 1):
-        ring_first(None, f2_ref.at[halves[part]], part)
+        ring_first(part)
     for k in (1, 2, 3):
         start(f1_ref, f1_full.at[zl, y], f1_send.at[2 + k], f1_recv.at[2 + k], at_y(k))
 
@@ -124,8 +140,8 @@
     fine = spread_matrix(128, 1, 0.25).astype(BF)
     coarse = [spread_matrix(128, 2, 1.0 / 16, 64 * j).astype(BF) for j in range(2)]
     both = [jnp.concatenate([fine, coarse[j]], axis=0) for j in range(2)]
-    ring_second(0, 0)
-    ring_second(0, 1)
+    ring_second(0)
+    ring_second(1)
 
     for k in (1, 2, 3):
         got = f1_full.at[(zl + 4 - k) % 4, y]
@@ -149,24 +165,61 @@
                 comb[rows, cols] = (comb[rows, cols].astype(F32) + upper).astype(BF)
         return 0
 
-    def other_first(part):
-        got = f2_full.at[(1 - zh) * 4 + x, halves[part]]
-        arrived(got, f2_send.at[part], f2_recv.at[part], across)
-        ring_first(1, got, part)
-
     steps = nq // 256
+    pass_piece(0)
     lax.fori_loop(0, steps // 2, merge, 0)
-    other_first(0)
-    other_first(1)
+    pass_piece(1)
     lax.fori_loop(steps // 2, steps, merge, 0)
+    pass_piece(2)
+    pass_piece(3)
+
+    def query_half(side):
+        channels = f2_full[pl.ds(4 * side, 4)].reshape(C // 2, nt)
+
+        def query(n, _):
+            rows = pl.ds(pl.multiple_of(n * 256, 256), 256)
+            part = mm(channels, comb[rows, :], 1, 1) * FACTOR
+            gq[pl.ds(2 * side, 2), :, :, rows] = part.astype(BF).reshape(2, 4, 16, 256)
+            return 0
+
+        lax.fori_loop(0, nq // 256, query, 0)
+
+    def query_scatter(p, side):
+        for k in (1, 2, 3):
+            i = 3 * p + k - 1
+            start(gq.at[pl.ds(2 * side, 2), (y + k) % 4], gq_in.at[p, k - 1], gq_send.at[i], gq_recv.at[i], at_y(k))
+
+    late = []
+
+    def query_total(p, side):
+        for k in (1, 2, 3):
+            i = 3 * p + k - 1
+            arrived(gq_in.at[p, k - 1], gq_send.at[i], gq_recv.at[i], at_y(k))
+        for j in (0, 1):
+            to = 2 * side + j
+            k = (to + 4 - zl) % 4
+            total = gq[to, y].astype(F32)
+            for m in range(3):
+                total = total + gq_in[p, m, j].astype(F32)
+            gq_out[2 * p + j] = total.astype(BF)
+            c = copy(
+                gq_out.at[2 * p + j], gq_in_z.at[(k + 3) % 4], gq_send.at[6 + (k + 3) % 4],
+                gq_recv.at[6 + (k + 3) % 4], (dp, pb, to * 4 + y),
+            )
+
+            @pl.when(to == zl)
+            def _():
+                gq_sum[...] = total
+
+            pl.when(to != zl)(c.start)
+            late.append((to, c))
+
 
     for k in (1, 2, 3):
         arrived(f1_full.at[zl, (y + 4 - k) % 4], f1_send.at[2 + k], f1_recv.at[2 + k], at_y(k))
         for m in (1, 2, 3):
             i = 3 + 3 * m + k - 1
             arrived(f1_full.at[(zl + 4 - m) % 4, (y + 4 - k) % 4], f1_send.at[i], f1_recv.at[i], at_y(k))
-    ring_second(1, 0)
-    ring_second(1, 1)
 
     first = f1_full[...].reshape(C, nq)
 
@@ -178,63 +231,46 @@
 
     lax.fori_loop(0, nt // W, target, 0)
 
-    def side_of(h):
-        return (1 - zh) if h == 0 else zh
-
-    def scatter_first(h):
-        base = 6 * h
-        for way, k in ((0, 1), (1, 3)):
+    spans = [(1 - zh, pl.ds(0, nt // 2)), (1 - zh, pl.ds(nt // 2, nt // 2)), (zh, pl.ds(0, nt))]
+
+    def scatter(n):
+        side, cols = spans[n]
+        for k in (1, 2, 3):
+            i = 3 * n + k - 1
             start(
-                gt.at[side_of(h), near(2), halves[way]], gt_in.at[h, way],
-                gt_send.at[base + way], gt_recv.at[base + way], at_x(k),
+                gt.at[side, near(k), :, cols], gt_in.at[n // 2, k - 1, :, cols],
+                gt_send.at[i], gt_recv.at[i], at_x(k),
             )
-        for way, k in ((0, 1), (1, 3)):
-            start(
-                gt.at[side_of(h), near(k), halves[1 - way]], gt_in.at[h, 2 + way],
-                gt_send.at[base + 2 + way], gt_recv.at[base + 2 + way], at_x(k),
-            )
-
-    def scatter_second(h):
-        base = 6 * h
-        for way, k in ((0, 1), (1, 3)):
-            arrived(gt_in.at[h, way], gt_send.at[base + way], gt_recv.at[base + way], at_x(k))
-            here = gt[side_of(h), near(k), halves[way], :].astype(F32)
-            gt_mid[h, way] = (here + gt_in[h, way].astype(F32)).astype(BF)
-            start(
-                gt_mid.at[h, way], gt_in.at[h, 4 + way],
-                gt_send.at[base + 4 + way], gt_recv.at[base + 4 + way], at_x(k),
-            )
-
-    def scatter_total(h, part):
-        base = 6 * h
-        total = gt[side_of(h), x, halves[part], :].astype(F32)
-        for way, k in ((0, 1), (1, 3)):
-            i = (4 if way == part else 2) + way
-            arrived(gt_in.at[h, i], gt_send.at[base + i], gt_recv.at[base + i], at_x(k))
-            total = total + gt_in[h, i].astype(F32)
+
+    def scatter_total(n):
+        side, cols = spans[n]
+        total = gt[side, x, :, cols].astype(F32)
+        for k in (1, 2, 3):
+            i = 3 * n + k - 1
+            arrived(gt_in.at[n // 2, k - 1, :, cols], gt_send.at[i], gt_recv.at[i], at_x(k))
+            total = total + gt_in[n // 2, k - 1, :, cols].astype(F32)
         return total
 
-    scatter_first(0)
-    scatter_first(1)
-
-    ring_rest(0)
-    ring_rest(1)
+    def cross(n):
+        cols = spans[n][1]
+        gt_out[:, cols] = scatter_total(n).astype(BF)
+        start(gt_out.at[:, cols], gt_in_z.at[:, cols], gt_send.at[9 + n], gt_recv.at[9 + n], across)
+
+    scatter(0)
+    scatter(1)
+    ring_rest()
+    query_half(zh)
+    query_scatter(0, zh)
+    await_pieces()
+    query_half(1 - zh)
+    query_scatter(1, 1 - zh)
+    scatter(2)
+    query_total(0, zh)
+    cross(0)
+    cross(1)
+    query_total(1, 1 - zh)
 
     second = f2_full[...].reshape(C, nt)
-
-    def query(n, _):
-        rows = pl.ds(pl.multiple_of(n * 256, 256), 256)
-        part = mm(second, comb[rows, :], 1, 1) * FACTOR
-        gq[:, :, :, rows] = part.astype(BF).reshape(4, 4, 16, 256)
-        return 0
-
-    lax.fori_loop(0, nq // 256, query, 0)
-    for k in (1, 2, 3):
-        start(gq.at[:, (y + k) % 4], gq_in.at[k - 1], gq_send.at[k - 1], gq_recv.at[k - 1], at_y(k))
-
-    scatter_second(0)
-    scatter_second(1)
-
     narrow = [spread_matrix(W // 2 ** l, l, 4.0 ** -l).astype(BF) for l in (1, 2, 3)]
     mean = jnp.concatenate(narrow + [jnp.zeros((32, W), BF)], axis=0)
     images = [mm(second[:, r * W:(r + 1) * W], mean, 1, 1) for r in range(8)]
@@ -266,33 +302,15 @@
 
     lax.fori_loop(0, nq // 256, volume, 0)
 
-    for part in (0, 1):
-        gt_out[halves[part], :] = scatter_total(0, part).astype(BF)
-        start(
-            gt_out.at[halves[part]], gt_in_z.at[halves[part]], gt_send.at[12 + part], gt_recv.at[12 + part], across
-        )
-
+    gt_sum[...] = scatter_total(2)
     for k in (1, 2, 3):
-        arrived(gq_in.at[k - 1], gq_send.at[k - 1], gq_recv.at[k - 1], at_y(k))
-    for k in (1, 2, 3, 0):
-        to = (zl + k) % 4
-        total = gq[to, y].astype(F32)
-        for m in range(3):
-            total = total + gq_in[m, to].astype(F32)
-        if k:
-            gq_out[k - 1] = total.astype(BF)
-            start(gq_out.at[k - 1], gq_in_z.at[k - 1], gq_send.at[2 + k], gq_recv.at[2 + k], at_zl(k))
-        else:
-            gq_sum[...] = total
-    for part in (0, 1):
-        gt_sum[halves[part], :] = scatter_total(1, part)
-
-    for k in (1, 2, 3):
-        arrived(gq_in_z.at[k - 1], gq_send.at[2 + k], gq_recv.at[2 + k], at_zl(k))
-    for part in (0, 1):
-        arrived(gt_in_z.at[halves[part]], gt_send.at[12 + part], gt_recv.at[12 + part], across)
+        arrived(gq_in_z.at[k - 1], gq_send.at[5 + k], gq_recv.at[5 + k], at_zl(k))
+    for n in (0, 1):
+        arrived(gt_in_z.at[:, spans[n][1]], gt_send.at[9 + n], gt_recv.at[9 + n], across)
     for c in sent:
         c.wait_send()
+    for to, c in late:
+        pl.when(to != zl)(c.wait_send)
 
 
 def finish(
@@ -349,21 +367,20 @@
             pltpu.VMEM((2, C, nt // 64), BF),
             pltpu.VMEM((2, 4, 32, nt), BF),
             pltpu.VMEM((4, 4, 16, nq), BF),
-            pltpu.VMEM((2, 6, 16, nt), BF),
-            pltpu.VMEM((2, 2, 16, nt), BF),
+            pltpu.VMEM((2, 3, 32, nt), BF),
             pltpu.VMEM((32, nt), BF),
-            pltpu.VMEM((3, 4, 16, nq), BF),
-            pltpu.VMEM((3, 16, nq), BF),
+            pltpu.VMEM((2, 3, 2, 16, nq), BF),
+            pltpu.VMEM((4, 16, nq), BF),
             dma((4,)),
             dma((2,)),
             dma((15,)),
             dma((15,)),
-            dma((14,)),
-            dma((14,)),
-            dma((14,)),
-            dma((14,)),
-            dma((6,)),
-            dma((6,)),
+            dma((22,)),
+            dma((22,)),
+            dma((11,)),
+            dma((11,)),
+            dma((9,)),
+            dma((9,)),
         ],
         compiler_params=pltpu.CompilerParams(
             collective_id=0, has_side_effects=True, vmem_limit_bytes=40 * 2**20

time: 47.1 us -> 43 us (0.913)
  Pallas kernels: 46.4 us -> 41.9 us
    pallas_call x1, Pallas kernels: 43.9 us -> 39.4 us  [body(): pl.pallas_call(exchange, out_shape=volumes + (sds((32, nt), F32), sds((32...]
where the time goes in v3:
time: 43 us; the launch traced here: 42.5 us
  Pallas kernels  41.9 us (97%)
  between operations  0.64 us (1%)
    pallas_call x1, Pallas kernels, body(): pl.pallas_call(exchange, out_shape=volumes + (sds((32, nt), F32), sds((32...  39.4 us
    pallas_call x1, Pallas kernels, body(): pl.pallas_call(finish, out_shape=volumes + (sds((16, nq), BF), sds((32, n...  2.52 us

profile of v3, /device:TPU:32, one launch (start us, length us, event | category | flops | bytes accessed | tf_op | source)
XLA Modules:
  0.0 42.5 jit_solution(463860384151628755)
XLA Ops:
  0.6 39.4 %exchange.1 = (bf16[1024,2048]{1,0:T(8,128)(2,1)S(1)}, bf16[1024,512]{1,0:T(8,128)(2,1)S(1)}, bf16[1024,128]{1,0:T(8,128)(2,1)S(1)}, bf16[32,1024]{1,0:T(8,128)(...) custom-call(bf16[16,1024]{1,0:T(8,128)(2,1)} %bitcast.10, ...), custom_call_target="tpu_custom_call" | custom-call | flops 5368709120 | bytes 16777216 | tf_op jit(solution)/shard_map/exchange/pallas_call | solution.py:348
  40.0 2.5 %finish.1 = (bf16[1024,2048]{1,0:T(8,128)(2,1)}, bf16[1024,512]{1,0:T(8,128)(2,1)}, bf16[1024,128]{1,0:T(8,128)(2,1)}, bf16[32,1024]{1,0:T(8,128)(2,1)}, bf16[16...) custom-call(bf16[1024,2048]{1,0:T(8,128)(2,1)S(1)} %get-tuple-element.20.v0, bf16[1024,512]{1,0:T(8,128)(2,1)S(1)} %get-tuple-element.21.v1, ...), custom_call_target="tpu_custom_call" | custom-call | bytes 8388608 | tf_op jit(solution)/shard_map/finish/pallas_call | solution.py:391
